TPU v7x, 32 devices: a whole 2x2x4 slice. The times are simulated.
32 devices in a mesh: dp: 8 (over z, core), tensor: 4 (over y, x).
Axes of the slice: x: 2, y: 2, z: 4, core: 2. Of those that a mesh axis runs over, the one named last changes fastest.
Arguments:
- queries: bfloat16 [1024, 8192], P('dp', 'tensor'), parts along dimension 0
- tree_states: bfloat16 [1024, 2048], P(('dp', 'tensor')), parts along dimension 0, may hold values from -6 to 6
- cache_codes: bfloat16 [640, 8, 2, 64, 128], P(('dp', 'tensor')), parts along dimension 0, may hold values from 0 to 255, as said below
- cache_scales: float32 [640, 8, 2, 128], P(('dp', 'tensor')), parts along dimension 0, may hold values from 0.3 to 3
- bit_widths: int32 [64], P('dp'), parts along dimension 0, may hold values from 2 to 8, as said below
- page_table: int32 [32, 20], P('dp'), parts along dimension 0, may hold values from 0 to 19, as said below
- lengths: int32 [32], P('dp'), parts along dimension 0, may hold values from 1 to 1280, as said below
- parents: int32 [32, 32], P('dp'), parts along dimension 0, may hold values from 0 to 30, as said below
- tree_mask: int32 [32, 32, 32], P('dp'), parts along dimension 0, may hold values from 0 to 1, as said below
- output_weight: bfloat16 [8192, 8192], P('tensor'), may hold values from -0.09375 to 0.09375
- residual: bfloat16 [1024, 8192], P('dp', 'tensor'), parts along dimension 0
- norm_gain: bfloat16 [8192], P('tensor'), may hold values from 0.099609375 to 1.8984375
- draft_weight: bfloat16 [8192, 2048], P('tensor'), may hold values from -0.09375 to 0.09375
Outputs:
- feature: bfloat16 [1024, 8192], P('dp', 'tensor'), parts along dimension 0
- draft_projection: bfloat16 [1024, 2048], P('dp', 'tensor'), parts along dimension 0
There are 8 independent parts, one for each index of `dp`. A program takes and returns all parts, laid end to end along the dimension named above; an argument that names none is the same for every part. Nothing has to cross between parts.
Inputs may be any that keep to these rules, and one draw needn't show every extreme that they name: `bit_widths`: every head holds 2, 4 or 8 bits. `cache_codes`: on KV head g every entry is a whole number from 0 to 2 to the power bit_widths[g], minus 1. `page_table`: for each c, the entries of columns c * 5 to (c + 1) * 5 - 1 over all requests form a permutation of 0 to 19: slots in the pool of tensor index c. `lengths`: some request of every part has exactly 1280 positions. parents[r, 0] = 0; for i > 0 the parent is below i, in node i's own block of 8 nodes, or in the first block when i is the first node of its block. tree_mask[r, i, j] = 1 exactly when j is i or an ancestor of i under parents.
All inputs are finite; a program needn't handle non-finite values.
Results may differ from a plain program's by a relative error of at most 0.012.
Values may be sent and summed in bfloat16 or wider, within the bound.
A program may use at most 128 MiB of HBM per device.

v0:
```python
import math

import jax
import jax.numpy as jnp
from jax import lax
from jax.sharding import PartitionSpec as P

D = 8192
HQ = 64
KVH = 8
HD = 128
NODES = 32
PAGE = 64
PAGES_DEV = 5
REQS = 4
ROWS = 128


masked_score = -1e30
epsilon = 1e-05


def dequantize(cache_codes, cache_scales, bit_widths):
    levels = jnp.exp2(bit_widths.astype(jnp.float32))[None, :, None, None, None]
    drawn = cache_codes.astype(jnp.float32)
    scaled = cache_scales[:, :, :, None, :]
    return (scaled * (2.0 * drawn - levels + 1.0) / levels).astype(jnp.bfloat16)


def block_partial(request_query, key_rows, value_rows, in_range):
    scores = jnp.einsum(
        "nkgd,ktd->nkgt", request_query, key_rows, preferred_element_type=jnp.float32
    ) / math.sqrt(HD)
    live = in_range[None, None, None, :]
    scores = jnp.where(live, scores, masked_score)
    block_max = jnp.max(scores, axis=-1)
    weights = jnp.where(live, jnp.exp(scores - block_max[..., None]), 0.0)
    block_sum = jnp.sum(weights, axis=-1)
    block_out = jnp.einsum(
        "nkgt,ktd->nkgd",
        weights.astype(jnp.bfloat16),
        value_rows,
        preferred_element_type=jnp.float32,
    )
    block_out = block_out / jnp.where(block_sum > 0, block_sum, 1.0)[..., None]
    return (block_max, block_sum, block_out.astype(jnp.bfloat16))


def page_rows(chosen, heads_held, block_span):
    key_rows = chosen[:, :, 0].transpose(1, 0, 2, 3).reshape(heads_held, block_span, HD)
    value_rows = chosen[:, :, 1].transpose(1, 0, 2, 3).reshape(heads_held, block_span, HD)
    return (key_rows, value_rows)


def shards(
    queries,
    tree_states,
    cache_codes,
    cache_scales,
    bit_widths,
    page_table,
    lengths,
    parents,
    tree_mask,
    output_weight,
    residual,
    norm_gain,
    draft_weight,
):
    position = lax.axis_index("tensor")
    heads_dev = queries.shape[1] // HD
    groups = HQ // KVH
    block_span = PAGES_DEV * PAGE
    dequant = dequantize(cache_codes, cache_scales, bit_widths)
    every_query, tree_all = (
        lax.all_gather(queries, "tensor", axis=1, tiled=True),
        lax.all_gather(tree_states, "tensor", axis=0, tiled=True),
    )

    def one_request(request):
        request_query = lax.dynamic_slice_in_dim(every_query, request * NODES, NODES, 0).reshape(
            NODES, KVH, groups, HD
        )
        request_pages = lax.dynamic_index_in_dim(page_table, request, 0, keepdims=False)
        slot_ids = lax.dynamic_slice_in_dim(request_pages, position * PAGES_DEV, PAGES_DEV)
        key_rows, value_rows = page_rows(jnp.take(dequant, slot_ids, axis=0), KVH, block_span)
        positions = position * block_span + jnp.arange(block_span, dtype=jnp.int32)
        block_max, block_sum, block_out = block_partial(
            request_query, key_rows, value_rows, positions < lengths[request]
        )
        return (
            block_out.reshape(NODES, HQ * HD),
            block_max.reshape(NODES, HQ),
            block_sum.reshape(NODES, HQ),
        )

    partial_out, maxima, partial_sum = lax.map(one_request, jnp.arange(REQS, dtype=jnp.int32))
    partial_out = partial_out.reshape(ROWS, HQ * HD)
    maxima = maxima.reshape(ROWS, HQ)
    partial_sum = partial_sum.reshape(ROWS, HQ)
    row_max = lax.pmax(maxima, "tensor")
    weight = jnp.exp(maxima - row_max) * partial_sum
    weighted = (weight[..., None] * partial_out.astype(jnp.float32).reshape(ROWS, HQ, HD)).reshape(
        ROWS, HQ * HD
    )
    numerator, denominator = (
        lax.psum_scatter(weighted, "tensor", scatter_dimension=1, tiled=True),
        lax.psum_scatter(weight, "tensor", scatter_dimension=1, tiled=True),
    )
    context_max = lax.dynamic_slice_in_dim(row_max, position * heads_dev, heads_dev, 1)
    context_max = context_max.reshape(REQS, NODES, heads_dev)
    numerator = numerator.reshape(REQS, NODES, heads_dev, HD)
    denominator = denominator.reshape(REQS, NODES, heads_dev)
    tree_keys = tree_all[:, : KVH * HD].reshape(ROWS, KVH, HD)
    tree_values = tree_all[:, KVH * HD :].reshape(ROWS, KVH, HD)
    head_ids = (position * heads_dev + jnp.arange(heads_dev, dtype=jnp.int32)) // groups
    own_keys = jnp.take(tree_keys, head_ids, axis=1).reshape(REQS, NODES, heads_dev, HD)
    own_values = jnp.take(tree_values, head_ids, axis=1).reshape(REQS, NODES, heads_dev, HD)
    local_query = queries.reshape(REQS, NODES, heads_dev, HD)
    allowed = (tree_mask > 0)[:, :, None, :]
    tree_scores = jnp.einsum(
        "rnhd,rjhd->rnhj", local_query, own_keys, preferred_element_type=jnp.float32
    ) / math.sqrt(HD)
    tree_scores = jnp.where(allowed, tree_scores, masked_score)
    overall = jnp.maximum(context_max, jnp.max(tree_scores, axis=-1))
    rescale = jnp.exp(context_max - overall)
    tree_weights = jnp.where(allowed, jnp.exp(tree_scores - overall[..., None]), 0.0)
    total_numerator = numerator * rescale[..., None] + jnp.einsum(
        "rnhj,rjhd->rnhd",
        tree_weights.astype(jnp.bfloat16),
        own_values,
        preferred_element_type=jnp.float32,
    )
    total_denominator = denominator * rescale + jnp.sum(tree_weights, axis=-1)
    attended = (
        (total_numerator / total_denominator[..., None])
        .astype(jnp.bfloat16)
        .reshape(ROWS, heads_dev * HD)
    )
    projected = lax.psum_scatter(
        jnp.dot(attended, output_weight, preferred_element_type=jnp.float32),
        "tensor",
        scatter_dimension=1,
        tiled=True,
    )
    feature = (residual.astype(jnp.float32) + projected).astype(jnp.bfloat16)
    squares = lax.psum(jnp.sum(jnp.square(feature.astype(jnp.float32)), axis=1), "tensor")
    inverse = lax.rsqrt(squares / D + epsilon)
    normed = (
        feature.astype(jnp.float32) * inverse[:, None] * norm_gain.astype(jnp.float32)[None, :]
    ).astype(jnp.bfloat16)
    row_ids = (jnp.arange(REQS, dtype=jnp.int32)[:, None] * NODES + parents).reshape(ROWS)
    chosen_rows = jnp.take(normed, row_ids, axis=0)
    drafted = lax.psum_scatter(
        jnp.dot(chosen_rows, draft_weight, preferred_element_type=jnp.float32),
        "tensor",
        scatter_dimension=1,
        tiled=True,
    )
    return (feature, drafted.astype(jnp.bfloat16))


def solution(mesh):
    placed = (
        P("dp", "tensor"),
        P(("dp", "tensor"), None),
        P(("dp", "tensor"), None, None, None, None),
        P(("dp", "tensor"), None, None, None),
        P("dp"),
        P("dp", None),
        P("dp"),
        P("dp", None),
        P("dp", None, None),
        P("tensor", None),
        P("dp", "tensor"),
        P("tensor"),
        P("tensor", None),
    )
    return jax.shard_map(
        shards,
        mesh=mesh,
        in_specs=placed,
        out_specs=(P("dp", "tensor"), P("dp", "tensor")),
        check_vma=False,
    )
```

profile of v0, /device:TPU:0, one launch (start us, length us, event | category | flops | bytes accessed | tf_op | source)
XLA Modules:
  0.0 326.3 jit_solution(2630048243865333530)
XLA Ops:
  8.7 7.5 %divide_convert_fusion.1 = bf16[20,8,2,64,128]{4,3,2,1,0:T(8,128)(2,1)} fusion(bf16[20,8,2,64,128]{4,3,2,1,0:T(8,128)(2,1)} %param.19, f32[8]{0:T(128)S(1)} %multiply_exponential_fusion, f32[20,8,2,128]{3,2,1,0:T(2,128)} %param.20), kind=kLoop, calls=%fused_computation.39 | loop fusion | flops 18350080 | bytes 10649632 | tf_op jit(solution)/shard_map/convert_element_type | solution.py:27
  16.2 31.7 %all-gather.2.cloned.1.call-done = bf16[128,8192]{1,0:T(8,128)(2,1)} async-done(((bf16[128,2048]{1,0:T(8,128)(2,1)}), bf16[128,8192]{1,0:T(8,128)(2,1)}) %all-gather.2.cloned.1.call-update) | async-done | bytes 2097168 | tf_op jit(solution)/shard_map/all_gather | solution.py:76
  47.9 73.4 %while.17 = (s32[]{:T(128)}, bf16[4,32,8192]{2,1,0:T(8,128)(2,1)}, f32[4,32,64]{2,1,0:T(8,128)S(1)}, f32[4,32,64]{2,1,0:T(8,128)S(1)}, s32[4]{0:T(128)S(1)}, /*i...) while((s32[]{:T(128)}, bf16[4,32,8192]{2,1,0:T(8,128)(2,1)}, ...), condition=%wide.region_3.4_spmd, body=%wide.region_0.3_spmd.sunk | while | flops 345245376 | bytes 26114212 | solution.py:97
  50.7 3.3 %gather_fusion = bf16[5,8,2,64,128]{4,3,2,1,0:T(8,128)(2,1)S(1)} fusion(bf16[20,8,2,64,128]{4,3,2,1,0:T(8,128)(2,1)} %get-tuple-element.343, s32[1024]{0:T(1024)S(1)} %pad_clamp_fusion.4), kind=kCustom, calls=%fused_computation.clone.1 | custom fusion | bytes 2621460 | tf_op jit(solution)/shard_map/while/body/eval_jaxpr/jit(_take)/gather | solution.py:86
  59.4 2.1 bitcast_reduce_fusion.2
  69.0 3.3 %gather_fusion = bf16[5,8,2,64,128]{4,3,2,1,0:T(8,128)(2,1)S(1)} fusion(bf16[20,8,2,64,128]{4,3,2,1,0:T(8,128)(2,1)} %get-tuple-element.343, s32[1024]{0:T(1024)S(1)} %pad_clamp_fusion.4), kind=kCustom, calls=%fused_computation.clone.1 | custom fusion | bytes 2621460 | tf_op jit(solution)/shard_map/while/body/eval_jaxpr/jit(_take)/gather | solution.py:86
  77.7 2.1 bitcast_reduce_fusion.2
  87.3 3.3 %gather_fusion = bf16[5,8,2,64,128]{4,3,2,1,0:T(8,128)(2,1)S(1)} fusion(bf16[20,8,2,64,128]{4,3,2,1,0:T(8,128)(2,1)} %get-tuple-element.343, s32[1024]{0:T(1024)S(1)} %pad_clamp_fusion.4), kind=kCustom, calls=%fused_computation.clone.1 | custom fusion | bytes 2621460 | tf_op jit(solution)/shard_map/while/body/eval_jaxpr/jit(_take)/gather | solution.py:86
  96.0 2.1 bitcast_reduce_fusion.2
  105.7 3.3 %gather_fusion = bf16[5,8,2,64,128]{4,3,2,1,0:T(8,128)(2,1)S(1)} fusion(bf16[20,8,2,64,128]{4,3,2,1,0:T(8,128)(2,1)} %get-tuple-element.343, s32[1024]{0:T(1024)S(1)} %pad_clamp_fusion.4), kind=kCustom, calls=%fused_computation.clone.1 | custom fusion | bytes 2621460 | tf_op jit(solution)/shard_map/while/body/eval_jaxpr/jit(_take)/gather | solution.py:86
  114.3 2.1 bitcast_reduce_fusion.2
  121.3 16.1 %pmax.7 = f32[128,64]{1,0:T(8,128)S(1)} all-reduce(f32[128,64]{1,0:T(8,128)S(1)} %bitcast.159), channel_id=1, replica_groups=mesh['dp'=8,'tensor'=4] {'tensor'}, use_global_device_ids=true, to_apply=%region_4.5 | all-reduce | flops 8192 | bytes 65536 | tf_op jit(solution)/shard_map/pmax | solution.py:101
  138.6 5.7 %bitcast_multiply_fusion = f32[128,8192]{1,0:T(8,128)} fusion(f32[16,8,64,128]{3,2,1,0:T(8,128)S(1)} %bitcast.144, bf16[4,32,8192]{2,1,0:T(8,128)(2,1)S(1)} %copy-done), kind=kLoop, calls=%fused_computation.40 | loop fusion | flops 2097152 | bytes 10485760 | tf_op jit(solution)/shard_map/mul | solution.py:103
  145.2 12.6 %all_gather.7 = bf16[128,2048]{1,0:T(8,128)(2,1)S(1)} all-gather(bf16[32,2048]{1,0:T(8,128)(2,1)S(1)} %copy-done.4), channel_id=1, replica_groups=mesh['dp'=8,'tensor'=4] {'tensor'}, dimensions={0}, use_global_device_ids=true | all-gather | bytes 655360 | tf_op jit(solution)/shard_map/all_gather | solution.py:77
  162.2 17.7 %all-reduce = f32[128,64]{1,0:T(8,128)S(1)} all-reduce(f32[128,64]{1,0:T(8,128)S(1)} %bitcast_multiply_fusion.1), channel_id=3, replica_groups=mesh['dp'=8,'tensor'=4] {'tensor'}, use_global_device_ids=true, to_apply=%region_7.9.clone | all-reduce | flops 8192 | bytes 65536
  180.4 20.2 %reduce-scatter.5.cloned.1.call-done = f32[128,2048]{1,0:T(8,128)} async-done(((f32[128,8192]{1,0:T(8,128)}), f32[128,2048]{1,0:T(8,128)}) %reduce-scatter.5.cloned.1.call-update) | async-done | bytes 1048592 | tf_op jit(solution)/shard_map/reduce_scatter | solution.py:107
  200.5 1.4 copy.111
  203.2 17.0 %fusion.34 = f32[128,8192]{1,0:T(8,128)} fusion(bf16[2048,8192]{1,0:T(8,128)(2,1)} %param.26, bf16[16,8,16,128]{3,2,1,0:T(8,128)(2,1)S(1)} %bitcast.148), kind=kOutput, calls=%fused_computation.58 | convolution fusion | flops 4294967296 | bytes 38273024 | tf_op jit(solution)/shard_map/dot_general | solution.py:141
  221.1 51.9 %reduce-scatter.7.cloned.1.call-done = f32[128,2048]{1,0:T(8,128)} async-done(((f32[128,8192]{1,0:T(8,128)}), f32[128,2048]{1,0:T(8,128)}) %reduce-scatter.7.cloned.1.call-update) | async-done | bytes 1048592 | tf_op jit(solution)/shard_map/reduce_scatter | solution.py:140
  273.0 1.5 fusion.28
  274.5 8.9 %psum.7 = f32[128]{0:T(128)S(1)} all-reduce(f32[128]{0:T(128)S(1)} %get-tuple-element.207), channel_id=1, replica_groups=mesh['dp'=8,'tensor'=4] {'tensor'}, use_global_device_ids=true, to_apply=%region_11.13 | all-reduce | flops 128 | bytes 1024 | tf_op jit(solution)/shard_map/psum | solution.py:147
  284.6 5.7 %fusion.40 = f32[128,2048]{1,0:T(8,128)} fusion(bf16[2048,2048]{1,0:T(8,128)(2,1)} %param.29, bf16[128,2048]{1,0:T(8,128)(2,1)S(1)} %gather_fusion.1, pred[128]{0:T(512)(128)(4,1)S(1)} %compare_and_fusion.2), kind=kOutput, calls=%fused_computation.64 | convolution fusion | flops 1074003968 | bytes 9961600 | tf_op jit(solution)/shard_map/dot_general | solution.py:155
  290.3 27.8 %reduce-scatter.9.cloned.1.call-done = f32[128,512]{1,0:T(8,128)} async-done(((f32[128,2048]{1,0:T(8,128)}), f32[128,512]{1,0:T(8,128)}) %reduce-scatter.9.cloned.1.call-update) | async-done | bytes 262160 | tf_op jit(solution)/shard_map/reduce_scatter | solution.py:154
  318.1 1.6 convert_element_type.68
  (157 shorter events, 51.5 us)
Async XLA Ops:
  7.2 40.7 %all-gather.2.cloned.1.call-start = ((), (), s32[]{:S(2)}) async-start(), calls=%async_computation.3 | async-start | bytes 2621440 | tf_op jit(solution)/shard_map/all_gather | solution.py:76
  7.9 192.6 %reduce-scatter.5.cloned.1.call-start = ((), (), s32[]{:S(2)}) async-start(), calls=%async_computation.4 | async-start | bytes 5242880 | tf_op jit(solution)/shard_map/reduce_scatter | solution.py:107
  8.6 39.2 %copy-start.6 = (s32[4,20]{1,0:T(4,128)S(1)}, s32[4,20]{1,0:T(4,128)}, u32[]{:S(2)}) copy-start(s32[4,20]{1,0:T(4,128)} %param.22) | copy-start | bytes 964
  8.6 39.2 %copy-start.9 = (s32[4]{0:T(128)S(1)}, s32[4]{0:T(128)}, u32[]{:S(2)}) copy-start(s32[4]{0:T(128)} %param.23) | copy-start | bytes 52
  121.3 17.3 %copy-start = (bf16[4,32,8192]{2,1,0:T(8,128)(2,1)S(1)}, bf16[4,32,8192]{2,1,0:T(8,128)(2,1)}, u32[]{:S(2)}) copy-start(bf16[4,32,8192]{2,1,0:T(8,128)(2,1)} %get-tuple-element.184) | copy-start | bytes 6291460
  144.3 0.9 copy-start.4
  144.3 15.6 %copy-start.5 = (s32[4,32,32]{2,1,0:T(8,128)S(1)}, s32[4,32,32]{2,1,0:T(8,128)}, u32[]{:S(2)}) copy-start(s32[4,32,32]{2,1,0:T(8,128)} %param.25) | copy-start | bytes 49156
  144.4 15.7 %copy-start.2 = (bf16[128,2048]{1,0:T(8,128)(2,1)S(1)}, bf16[128,2048]{1,0:T(8,128)(2,1)}, u32[]{:S(2)}) copy-start(bf16[128,2048]{1,0:T(8,128)(2,1)} %param.17) | copy-start | bytes 1572868
  144.4 128.7 %reduce-scatter.7.cloned.1.call-start = ((), (), s32[]{:S(2)}) async-start(), calls=%async_computation.5 | async-start | bytes 5242880 | tf_op jit(solution)/shard_map/reduce_scatter | solution.py:140
  157.8 2.4 copy-start.10
  220.2 0.7 copy-start.8
  220.2 0.9 copy-start.7
  220.2 52.9 %copy-start.3 = (bf16[128,2048]{1,0:T(8,128)(2,1)S(1)}, bf16[128,2048]{1,0:T(8,128)(2,1)}, u32[]{:S(2)}) copy-start(bf16[128,2048]{1,0:T(8,128)(2,1)} %param.27) | copy-start | bytes 1572868
  220.2 97.9 %reduce-scatter.9.cloned.1.call-start = ((), (), s32[]{:S(2)}) async-start(), calls=%async_computation.6 | async-start | bytes 1310720 | tf_op jit(solution)/shard_map/reduce_scatter | solution.py:154
  274.5 15.8 %copy-start.1 = (bf16[128,2048]{1,0:T(8,128)(2,1)}, bf16[128,2048]{1,0:T(8,128)(2,1)S(1)}, u32[]{:S(2)}) copy-start(bf16[128,2048]{1,0:T(8,128)(2,1)S(1)} %get-tuple-element.208) | copy-start | bytes 1572868
Sparse Core Ops, SparseCore 0:
  9.8 38.0 all-gather.1
  144.5 56.0 reduce-scatter.4
  220.3 52.6 reduce-scatter.6
  290.4 27.6 reduce-scatter.8
where the time goes:
time: 328 us; the launch traced here: 326 us
  waiting for transfers between devices  132 us (40%)
  blocking collectives  55.3 us (17%)
  local copies, waits for them, and re-layouts  49.2 us (15%)
  matrix products  37 us (11%)
  other arithmetic  26.2 us (8%)
  between operations  14.7 us (4%)
  loops' own time  11.3 us (3%)
    reduce_scatter x1, waiting for transfers between devices, shards(): lax.psum_scatter(jnp.dot(attended, output_weight, preferred_element_type=...  51.9 us
    all_gather x1, waiting for transfers between devices, shards(): lax.all_gather(queries, 'tensor', axis=1, tiled=True)  31.7 us
    reduce_scatter x1, waiting for transfers between devices, shards(): lax.psum_scatter(jnp.dot(chosen_rows, draft_weight, preferred_element_typ...  27.8 us
    reduce_scatter x1, waiting for transfers between devices, shards(): lax.psum_scatter(weighted, 'tensor', scatter_dimension=1, tiled=True)  20.2 us
    unnamed x1, blocking collectives  17.7 us
    dot_general x1, matrix products, shards(): jnp.dot(attended, output_weight, preferred_element_type=jnp.float32)  17 us
    pmax x1, blocking collectives, shards(): row_max = lax.pmax(maxima, 'tensor')  16.1 us
    gather x4, local copies, waits for them, and re-layouts, one_request(): jnp.take(dequant, slot_ids, axis=0)  13.1 us
  transfers between devices with their start and end apart: 4, of which 4 were waited for; matrix products, arithmetic and copies ran while one was open for 4% of the time, Pallas kernels for 0%

commit v1 on v0

v1 whole, which is shorter than its diff:
```python
import functools
import math

import jax
import jax.numpy as jnp
from jax import lax
from jax.experimental import pallas as pl
from jax.experimental.pallas import tpu as pltpu
from jax.sharding import PartitionSpec as P

MESH = pl.DeviceIdType.MESH
masked_score = -1e30
epsilon = 1e-05


def attend(stacked, keys, values, live, scale):
    scores = lax.dot_general(
        stacked, keys, (((1,), (1,)), ((), ())), preferred_element_type=jnp.float32
    ) * scale
    scores = jnp.where(live, scores, masked_score)
    top = jnp.max(scores, axis=1, keepdims=True)
    weights = jnp.where(live, jnp.exp(scores - top), 0.0)
    total = jnp.sum(weights, axis=1, keepdims=True)
    mixed = jnp.dot(weights.astype(jnp.bfloat16), values, preferred_element_type=jnp.float32)
    return top, total, mixed / jnp.where(total > 0, total, 1.0)


def kernel(
    n,
    chunks,
    groups,
    q_ref,
    tree_ref,
    scales_ref,
    bits_ref,
    table_ref,
    lengths_ref,
    parents_ref,
    mask_ref,
    residual_ref,
    gain_ref,
    codes_hbm,
    weight_hbm,
    draft_hbm,
    feature_ref,
    drafted_ref,
    cache,
    weight,
    draft,
    q_all,
    t_send,
    t_all,
    b_send,
    b_recv,
    s_send,
    s_recv,
    t_out,
    t_stat,
    attended,
    c_send,
    c_recv,
    own,
    scaled,
    d_send,
    d_recv,
    d_own,
    sq_send,
    sq_recv,
    local_sem,
    weight_sem,
    draft_sem,
    q_sems,
    t_sems,
    b_sems,
    s_sems,
    c_sems,
    d_sems,
    sq_sems,
):
    me = lax.axis_index("tensor")
    rows, width = q_ref.shape
    slots, kv_heads, _, page, hd = cache.shape
    requests = lengths_ref.shape[0]
    nodes = rows // requests
    per = requests // chunks
    span = per * nodes
    heads = width // hd
    gh = min(groups, heads)
    kv_dev = heads // gh
    pages = table_ref.shape[1] // n
    block = pages * page
    tree_rows = tree_ref.shape[0]
    tree_width = kv_dev * hd
    out_width = draft.shape[2]
    scale = 1.0 / math.sqrt(hd)
    half = 128 // 2
    f32, bf16 = jnp.float32, jnp.bfloat16

    def ahead(k):
        return lax.rem(me + k, n)

    def behind(k):
        return lax.rem(me + n - k, n)

    def remote(src, dst, sems, index, k):
        return pltpu.make_async_remote_copy(
            src_ref=src,
            dst_ref=dst,
            send_sem=sems.at[(0, *index)],
            recv_sem=sems.at[(1, *index)],
            device_id={"tensor": ahead(k)},
            device_id_type=MESH,
        )

    def send_q(c, k):
        return remote(q_all.at[c, 0], q_all.at[c, k], q_sems, (c, k), k)

    def send_t(k):
        at = pl.ds(pl.multiple_of(me * tree_rows, tree_rows), tree_rows)
        return remote(t_send.at[k], t_all.at[:, at, :], t_sems, (k,), k)

    def send_b(c, k):
        return remote(b_send.at[c, n - k], b_recv.at[c, k], b_sems, (c, k), k)

    def send_s(c, k):
        return remote(s_send.at[c, n - k], s_recv.at[c, k], s_sems, (c, k), k)

    def send_c(c, k):
        return remote(c_send.at[c, k], c_recv.at[c, k], c_sems, (c, k), k)

    def send_d(c, k):
        return remote(d_send.at[c, k], d_recv.at[c, k], d_sems, (c, k), k)

    def send_sq(c, k):
        return remote(sq_send.at[c], sq_recv.at[c, k], sq_sems, (c, k), k)

    def load_weight(k):
        at = pl.ds(pl.multiple_of(ahead(k) * width, width), width)
        return pltpu.make_async_copy(weight_hbm.at[:, at], weight.at[k], weight_sem.at[k])

    def load_draft(k):
        at = pl.ds(pl.multiple_of(ahead(k) * out_width, out_width), out_width)
        return pltpu.make_async_copy(draft_hbm.at[:, at], draft.at[k], draft_sem.at[k])

    load_cache = pltpu.make_async_copy(codes_hbm, cache, local_sem)
    load_cache.start()

    barrier = pltpu.get_barrier_semaphore()
    for k in range(1, n):
        pl.semaphore_signal(
            barrier, inc=1, device_id={"tensor": ahead(k)}, device_id_type=MESH
        )
    for c in range(chunks):
        q_all[c, 0] = q_ref[c * span : (c + 1) * span, :]
    for k in range(n):
        first = ahead(k) * heads // groups
        for part in range(2):
            at = pl.ds(pl.multiple_of((part * kv_heads + first) * hd, hd), tree_width)
            t_send[k, part] = tree_ref[:, at].astype(t_send.dtype)
    mine = pl.ds(pl.multiple_of(me * tree_rows, tree_rows), tree_rows)
    t_all[:, mine, :] = t_send[0]
    pl.semaphore_wait(barrier, n - 1)

    for c in range(chunks):
        for k in range(1, n):
            send_q(c, k).start()
    for k in range(1, n):
        send_t(k).start()
    for k in range(n):
        load_weight(k).start()
    for k in range(n):
        load_draft(k).start()

    load_cache.wait()

    @pl.loop(0, slots)
    def _(slot):
        for g in range(kv_heads):
            level = jnp.full((1, hd), jnp.left_shift(jnp.int32(1), bits_ref[g]), jnp.int32)
            level = level.astype(f32)
            for part in range(2):
                ratio = scales_ref[slot, g, part : part + 1, :] / level
                codes = cache[slot, g, part].astype(f32)
                cache[slot, g, part] = (ratio * (2.0 * codes - level + 1.0)).astype(bf16)

    lane = lax.broadcasted_iota(jnp.int32, (nodes, 128), 1)
    place = lax.broadcasted_iota(jnp.int32, (1, block), 1) + me * block

    def stack(c, k, r, j):
        at = slice(r * nodes, (r + 1) * nodes)
        cols = [slice((j * gh + h) * hd, (j * gh + h + 1) * hd) for h in range(gh)]
        return jnp.concatenate([q_all[c, k, at, col] for col in cols], axis=0)

    def add_stats(stats, r, j, top, total):
        for h in range(gh):
            at = r * heads + j * gh + h
            part = slice(h * nodes, (h + 1) * nodes)
            stats = jnp.where(lane == at, top[part], stats)
            stats = jnp.where(lane == half + at, total[part], stats)
        return stats

    @pl.loop(0, chunks)
    def _(c):
        @pl.loop(0, n)
        def _(k):
            @pl.when(k > 0)
            def _():
                send_q(c, k).wait_recv()

            first = behind(k) * heads // groups
            stats = jnp.zeros((nodes, 128), f32)
            for r in range(per):
                request = c * per + r
                ids = [table_ref[request, me * pages + p] for p in range(pages)]
                live = place < lengths_ref[request]
                for j in range(kv_dev):
                    keys, values = (
                        jnp.concatenate([cache[i, first + j, part] for i in ids], axis=0)
                        for part in range(2)
                    )
                    top, total, mixed = attend(stack(c, k, r, j), keys, values, live, scale)
                    stats = add_stats(stats, r, j, top, total)
                    mixed = mixed.astype(bf16)
                    for h in range(gh):
                        b_send[
                            c,
                            k,
                            r * nodes : (r + 1) * nodes,
                            (j * gh + h) * hd : (j * gh + h + 1) * hd,
                        ] = mixed[h * nodes : (h + 1) * nodes]
            s_send[c, k] = stats

            @pl.when(k > 0)
            def _():
                send_b(c, n - k).start()
                send_s(c, n - k).start()

    for k in range(1, n):
        send_t(k).wait_recv()

    @pl.loop(0, chunks)
    def _(c):
        stats = jnp.zeros((nodes, 128), f32)
        for r in range(per):
            request = c * per + r
            allowed = jnp.concatenate([mask_ref[request]] * gh, axis=0) > 0
            at = pl.ds(pl.multiple_of(request * nodes, nodes), nodes)
            for j in range(kv_dev):
                col = slice(j * hd, (j + 1) * hd)
                keys, values = (t_all[part, at, col].astype(bf16) for part in range(2))
                top, total, mixed = attend(stack(c, 0, r, j), keys, values, allowed, scale)
                stats = add_stats(stats, r, j, top, total)
                for h in range(gh):
                    t_out[
                        c,
                        r * nodes : (r + 1) * nodes,
                        (j * gh + h) * hd : (j * gh + h + 1) * hd,
                    ] = mixed[h * nodes : (h + 1) * nodes]
        t_stat[c] = stats

    for k in range(n):
        load_weight(k).wait()

    tile = min(width, 512)

    @pl.loop(0, chunks)
    def _(c):
        for k in range(1, n):
            send_b(c, k).wait_recv()
            send_s(c, k).wait_recv()
        stats = [t_stat[c], s_send[c, 0]] + [s_recv[c, k] for k in range(1, n)]
        overall = functools.reduce(jnp.maximum, stats)
        shares = [jnp.exp(one - overall) * pltpu.roll(one, half, 1) for one in stats]
        inverse = 1.0 / functools.reduce(jnp.add, shares)
        shares = [one * inverse for one in shares]
        for r in range(per):
            at = slice(r * nodes, (r + 1) * nodes)
            for h in range(heads):
                col = slice(h * hd, (h + 1) * hd)
                i = r * heads + h
                blocks = [t_out[c, at, col], b_send[c, 0, at, col].astype(f32)]
                blocks += [b_recv[c, k, at, col].astype(f32) for k in range(1, n)]
                mixed = functools.reduce(
                    jnp.add, [one[:, i : i + 1] * b for one, b in zip(shares, blocks)]
                )
                attended[at, col] = mixed.astype(bf16)

        @pl.loop(1, n)
        def _(k):
            @pl.loop(0, width // tile)
            def _(j):
                cols = pl.ds(pl.multiple_of(j * tile, tile), tile)
                c_send[c, k, :, cols] = jnp.dot(
                    attended[...], weight[k, :, cols], preferred_element_type=f32
                ).astype(bf16)

            send_c(c, k).start()

        @pl.loop(0, width // tile)
        def _(j):
            cols = pl.ds(pl.multiple_of(j * tile, tile), tile)
            own[c, :, cols] = jnp.dot(
                attended[...], weight[0, :, cols], preferred_element_type=f32
            )

    for k in range(n):
        load_draft(k).wait()

    row_of = lax.broadcasted_iota(jnp.int32, (span, 128), 0)
    lane_of = lax.broadcasted_iota(jnp.int32, (span, 128), 1)
    diagonal = row_of == lane_of

    @pl.loop(0, chunks)
    def _(c):
        for k in range(1, n):
            send_c(c, k).wait_recv()
        at = pl.ds(pl.multiple_of(c * span, span), span)

        def finish(j, squares):
            cols = pl.ds(pl.multiple_of(j * 128, 128), 128)
            total = own[c, :, cols]
            for k in range(1, n):
                total = total + c_recv[c, k, :, cols].astype(f32)
            feature = (residual_ref[at, cols].astype(f32) + total).astype(bf16)
            feature_ref[at, cols] = feature
            feature = feature.astype(f32)
            scaled[:, cols] = (feature * gain_ref[:, cols].astype(f32)).astype(bf16)
            return squares + feature * feature

        squares = lax.fori_loop(0, width // 128, finish, jnp.zeros((span, 128), f32))
        column = jnp.sum(squares, axis=1, keepdims=True)
        line = jnp.sum(jnp.where(diagonal, column, 0.0), axis=0, keepdims=True)
        sq_send[c] = jnp.broadcast_to(line, (8, 128))
        for k in range(1, n):
            send_sq(c, k).start()

        @pl.loop(1, n)
        def _(k):
            d_send[c, k] = jnp.dot(
                scaled[...], draft[k], preferred_element_type=f32
            ).astype(bf16)
            send_d(c, k).start()

        d_own[c] = jnp.dot(scaled[...], draft[0], preferred_element_type=f32)

    @pl.loop(0, chunks)
    def _(c):
        for k in range(1, n):
            send_sq(c, k).wait_recv()
            send_d(c, k).wait_recv()
        total = d_own[c]
        line = sq_send[c, 0:1, :]
        for k in range(1, n):
            total = total + d_recv[c, k].astype(f32)
            line = line + sq_recv[c, k, 0:1, :]
        column = jnp.sum(jnp.where(diagonal, line, 0.0), axis=1, keepdims=True)
        inverse = lax.rsqrt(column / (width * n) + epsilon)
        drafted = (total * inverse).astype(bf16)
        source = lax.broadcasted_iota(jnp.int32, (nodes, nodes), 0)
        for r in range(per):
            request = c * per + r
            chosen = (source == parents_ref[pl.ds(request, 1), :]).astype(f32).astype(bf16)
            moved = lax.dot_general(
                chosen,
                drafted[r * nodes : (r + 1) * nodes],
                (((0,), (0,)), ((), ())),
                preferred_element_type=f32,
            )
            to = pl.ds(pl.multiple_of(request * nodes, nodes), nodes)
            drafted_ref[to, :] = moved.astype(bf16)

    for k in range(1, n):
        send_t(k).wait_send()
        for c in range(chunks):
            for send in (send_q, send_b, send_s, send_c, send_d, send_sq):
                send(c, k).wait_send()


def shards(
    n,
    query_heads,
    queries,
    tree_states,
    cache_codes,
    cache_scales,
    bit_widths,
    page_table,
    lengths,
    parents,
    tree_mask,
    output_weight,
    residual,
    norm_gain,
    draft_weight,
):
    rows, width = queries.shape
    slots, kv_heads, _, page, hd = cache_codes.shape
    requests = lengths.shape[0]
    nodes = rows // requests
    groups = query_heads // kv_heads
    heads = width // hd
    chunks = 2 if requests % 2 == 0 else 1
    while requests // chunks * heads > 64 or requests // chunks * nodes > 128:
        chunks *= 2
    span = rows // chunks
    kv_dev = max(1, heads // groups)
    tree_rows = tree_states.shape[0]
    wire = jnp.bfloat16 if tree_rows % 16 == 0 else jnp.float32
    out_width = draft_weight.shape[1] // n
    f32, bf16 = jnp.float32, jnp.bfloat16
    dma = pltpu.SemaphoreType.DMA
    vmem, smem, hbm = (
        pl.BlockSpec(memory_space=space) for space in (pltpu.VMEM, pltpu.SMEM, pl.ANY)
    )
    sems = dma((2, chunks, n))
    return pl.pallas_call(
        functools.partial(kernel, n, chunks, groups),
        out_shape=(
            jax.ShapeDtypeStruct((rows, width), bf16),
            jax.ShapeDtypeStruct((rows, out_width), bf16),
        ),
        in_specs=[vmem, vmem, vmem, smem, smem, smem, vmem, vmem, vmem, vmem, hbm, hbm, hbm],
        out_specs=(vmem, vmem),
        scratch_shapes=[
            pltpu.VMEM(cache_codes.shape, bf16),
            pltpu.VMEM((n, width, width), bf16),
            pltpu.VMEM((n, width, out_width), bf16),
            pltpu.VMEM((chunks, n, span, width), bf16),
            pltpu.VMEM((n, 2, tree_rows, kv_dev * hd), wire),
            pltpu.VMEM((2, rows, kv_dev * hd), wire),
            pltpu.VMEM((chunks, n, span, width), bf16),
            pltpu.VMEM((chunks, n, span, width), bf16),
            pltpu.VMEM((chunks, n, nodes, 128), f32),
            pltpu.VMEM((chunks, n, nodes, 128), f32),
            pltpu.VMEM((chunks, span, width), f32),
            pltpu.VMEM((chunks, nodes, 128), f32),
            pltpu.VMEM((span, width), bf16),
            pltpu.VMEM((chunks, n, span, width), bf16),
            pltpu.VMEM((chunks, n, span, width), bf16),
            pltpu.VMEM((chunks, span, width), f32),
            pltpu.VMEM((span, width), bf16),
            pltpu.VMEM((chunks, n, span, out_width), bf16),
            pltpu.VMEM((chunks, n, span, out_width), bf16),
            pltpu.VMEM((chunks, span, out_width), f32),
            pltpu.VMEM((chunks, 8, 128), f32),
            pltpu.VMEM((chunks, n, 8, 128), f32),
            dma,
            dma((n,)),
            dma((n,)),
            sems,
            dma((2, n)),
            sems,
            sems,
            sems,
            sems,
            sems,
        ],
        compiler_params=pltpu.CompilerParams(
            collective_id=0, has_side_effects=True, vmem_limit_bytes=63 * 1024 * 1024
        ),
    )(
        queries,
        tree_states,
        cache_scales,
        bit_widths,
        page_table,
        lengths,
        parents,
        tree_mask,
        residual,
        norm_gain.reshape(1, -1),
        cache_codes,
        output_weight,
        draft_weight,
    )


def solution(mesh):
    n = mesh.shape["tensor"]
    placed = (
        P("dp", "tensor"),
        P(("dp", "tensor"), None),
        P(("dp", "tensor"), None, None, None, None),
        P(("dp", "tensor"), None, None, None),
        P("dp"),
        P("dp", None),
        P("dp"),
        P("dp", None),
        P("dp", None, None),
        P("tensor", None),
        P("dp", "tensor"),
        P("tensor"),
        P("tensor", None),
    )

    def run(*arrays):
        query_heads = arrays[0].shape[1] // arrays[2].shape[-1]
        return jax.shard_map(
            functools.partial(shards, n, query_heads),
            mesh=mesh,
            in_specs=placed,
            out_specs=(P("dp", "tensor"), P("dp", "tensor")),
            check_vma=False,
        )(*arrays)

    return run
```

time: 328 us -> 91.3 us (0.28)
  waiting for transfers between devices: 132 us -> 0 us
  Pallas kernels: 0 us -> 85.7 us
  blocking collectives: 55.3 us -> 0 us
  local copies, waits for them, and re-layouts: 49.2 us -> 4.74 us
  matrix products: 37 us -> 0 us
  other arithmetic: 26.2 us -> 0 us
  between operations: 14.7 us -> 0.64 us
  loops' own time: 11.3 us -> 0 us
    reduce_scatter x3 -> x0, waiting for transfers between devices: 99.9 us -> none  [the longest x1 51.9 us: shards(): lax.psum_scatter(jnp.dot(attended, output_weight, preferred_element_type=...]
    pallas_call x0 -> x1, Pallas kernels: none -> 85.7 us  [shards(): pl.pallas_call(functools.partial(kernel, n, chunks, groups), out_shape=(j...]
    dot_general x12 -> x0, matrix products: 37 us -> none  [the longest x1 17 us: shards(): jnp.dot(attended, output_weight, preferred_element_type=jnp.float32)]
    all_gather x1 -> x0, waiting for transfers between devices: 31.7 us -> none  [shards(): lax.all_gather(queries, 'tensor', axis=1, tiled=True)]
    unnamed x1 -> x0, blocking collectives: 17.7 us -> none
    pmax x1 -> x0, blocking collectives: 16.1 us -> none  [shards(): row_max = lax.pmax(maxima, 'tensor')]
    gather x7 -> x0, local copies, waits for them, and re-layouts: 15.4 us -> none  [the longest x4 13.1 us: one_request(): jnp.take(dequant, slot_ids, axis=0)]
    all_gather x1 -> x0, blocking collectives: 12.6 us -> none  [shards(): lax.all_gather(tree_states, 'tensor', axis=0, tiled=True)]
  transfers between devices with their start and end apart: 4 -> 0, of which waited for: 4 -> 0; matrix products, arithmetic and copies ran while one was open for 4% -> 0% of each run, Pallas kernels for 0% -> 0%
where the time goes in v1:
time: 91.3 us; the launch traced here: 91.1 us
  Pallas kernels  85.7 us (94%)
  local copies, waits for them, and re-layouts  4.74 us (5%)
    pallas_call x1, Pallas kernels, shards(): pl.pallas_call(functools.partial(kernel, n, chunks, groups), out_shape=(j...  85.7 us
    unnamed x2, local copies, waits for them, and re-layouts  3.45 us

profile of v1, /device:TPU:0, one launch (start us, length us, event | category | flops | bytes accessed | tf_op | source)
XLA Modules:
  0.0 91.1 jit_solution(4998818071833826051)
XLA Ops:
  0.6 1.3 %reshape.7.gain_ref = bf16[1,2048]{1,0:T(2,128)(2,1)} reshape(bf16[2048]{0:T(1024)(128)(2,1)} %param.24) | data formatting | bytes 8192 | tf_op jit(solution)/shard_map/reshape | solution.py:471
  1.9 85.7 %shard_map.140 = (bf16[128,2048]{1,0:T(8,128)(2,1)}, bf16[128,512]{1,0:T(8,128)(2,1)}) custom-call(bf16[128,2048]{1,0:T(8,128)(2,1)} %q_ref.1, bf16[32,2048]{1,0:T(8,128)(2,1)} %tree_ref.1, f32[20,8,2,128]{3,2,1,0:T(2,128)} %scales_ref.1, s32[8]{0:T(128)} %bits_ref.1, s32[4,20]{1,0:T(4,128)} %table_ref.1, s32[4]{0:T(128)} %lengths_ref.1, ...), custom_call_target="tpu_custom_call" | custom-call | tf_op jit(solution)/shard_map/pallas_call | solution.py:416
  87.7 1.9 %copy.17 = bf16[128,2048]{1,0:T(8,128)(2,1)} copy(bf16[128,2048]{1,0:T(8,128)(2,1)} %get-tuple-element.4) | data formatting | bytes 1048576
  89.5 1.6 %copy.18 = bf16[128,512]{1,0:T(8,128)(2,1)} copy(bf16[128,512]{1,0:T(8,128)(2,1)} %get-tuple-element.5) | data formatting | bytes 262144

commit v2 on v1

--- a/solution.py
+++ b/solution.py
@@ -66,6 +66,7 @@
     d_own,
     sq_send,
     sq_recv,
+    gain,
     local_sem,
     weight_sem,
     draft_sem,
@@ -96,11 +97,21 @@
     half = 128 // 2
     f32, bf16 = jnp.float32, jnp.bfloat16
 
+    relay = n == 4
+    part_rows = span // 2
+
+    def flipped(k):
+        low = lax.rem(me + k, 2)
+        return 2 * lax.rem(me // 2 + k // 2, 2) + low
+
     def ahead(k):
-        return lax.rem(me + k, n)
+        return flipped(k) if relay else lax.rem(me + k, n)
 
     def behind(k):
-        return lax.rem(me + n - k, n)
+        return flipped(k) if relay else lax.rem(me + n - k, n)
+
+    def back(k):
+        return k if relay else n - k
 
     def remote(src, dst, sems, index, k):
         return pltpu.make_async_remote_copy(
@@ -115,15 +126,31 @@
     def send_q(c, k):
         return remote(q_all.at[c, 0], q_all.at[c, k], q_sems, (c, k), k)
 
+    def forward_q(c, i):
+        rows_at = pl.ds(i * part_rows, part_rows)
+        return remote(
+            q_all.at[c, 1 + i, rows_at],
+            q_all.at[c, 3, rows_at],
+            q_sems,
+            (c, 3 - 3 * i),
+            2 - i,
+        )
+
+    def pass_c(c, i):
+        rows_at = pl.ds(i * part_rows, part_rows)
+        return remote(
+            c_send.at[c, 3, rows_at], c_recv.at[c, 3, rows_at], c_sems, (c, 3 - 3 * i), 1 + i
+        )
+
     def send_t(k):
         at = pl.ds(pl.multiple_of(me * tree_rows, tree_rows), tree_rows)
         return remote(t_send.at[k], t_all.at[:, at, :], t_sems, (k,), k)
 
     def send_b(c, k):
-        return remote(b_send.at[c, n - k], b_recv.at[c, k], b_sems, (c, k), k)
+        return remote(b_send.at[c, back(k)], b_recv.at[c, k], b_sems, (c, k), k)
 
     def send_s(c, k):
-        return remote(s_send.at[c, n - k], s_recv.at[c, k], s_sems, (c, k), k)
+        return remote(s_send.at[c, back(k)], s_recv.at[c, k], s_sems, (c, k), k)
 
     def send_c(c, k):
         return remote(c_send.at[c, k], c_recv.at[c, k], c_sems, (c, k), k)
@@ -144,6 +171,7 @@
 
     load_cache = pltpu.make_async_copy(codes_hbm, cache, local_sem)
     load_cache.start()
+    gain[...] = gain_ref[...].astype(f32)
 
     barrier = pltpu.get_barrier_semaphore()
     for k in range(1, n):
@@ -161,8 +189,9 @@
     t_all[:, mine, :] = t_send[0]
     pl.semaphore_wait(barrier, n - 1)
 
+    near = range(1, 3 if relay else n)
     for c in range(chunks):
-        for k in range(1, n):
+        for k in near:
             send_q(c, k).start()
     for k in range(1, n):
         send_t(k).start()
@@ -199,13 +228,37 @@
             stats = jnp.where(lane == half + at, total[part], stats)
         return stats
 
-    @pl.loop(0, chunks)
-    def _(c):
-        @pl.loop(0, n)
-        def _(k):
-            @pl.when(k > 0)
-            def _():
-                send_q(c, k).wait_recv()
+    def receive_q(c):
+        for k in (1, 2):
+            send_q(c, k).wait_recv()
+        for i in range(2):
+            forward_q(c, i).start()
+
+    @pl.loop(0, chunks * n)
+    def _(step):
+        later = jnp.maximum(step - chunks, 0)
+        own_step = step < chunks
+        c = jnp.where(own_step, step, later // (n - 1))
+        k = jnp.where(own_step, 0, 1 + lax.rem(later, n - 1))
+
+        if n > 0:
+            if relay:
+                @pl.when(step == chunks)
+                def _():
+                    receive_q(0)
+
+                @pl.when(k == 3)
+                def _():
+                    @pl.when(c < chunks - 1)
+                    def _():
+                        receive_q(c + 1)
+
+                    for i in range(2):
+                        forward_q(c, i).wait_recv()
+            else:
+                @pl.when(k > 0)
+                def _():
+                    send_q(c, k).wait_recv()
 
             first = behind(k) * heads // groups
             stats = jnp.zeros((nodes, 128), f32)
@@ -232,8 +285,8 @@
 
             @pl.when(k > 0)
             def _():
-                send_b(c, n - k).start()
-                send_s(c, n - k).start()
+                send_b(c, back(k)).start()
+                send_s(c, back(k)).start()
 
     for k in range(1, n):
         send_t(k).wait_recv()
@@ -285,23 +338,45 @@
                 )
                 attended[at, col] = mixed.astype(bf16)
 
-        @pl.loop(1, n)
-        def _(k):
+        def project(k, store):
             @pl.loop(0, width // tile)
             def _(j):
                 cols = pl.ds(pl.multiple_of(j * tile, tile), tile)
-                c_send[c, k, :, cols] = jnp.dot(
-                    attended[...], weight[k, :, cols], preferred_element_type=f32
-                ).astype(bf16)
-
-            send_c(c, k).start()
-
-        @pl.loop(0, width // tile)
-        def _(j):
-            cols = pl.ds(pl.multiple_of(j * tile, tile), tile)
-            own[c, :, cols] = jnp.dot(
-                attended[...], weight[0, :, cols], preferred_element_type=f32
-            )
+                store(
+                    cols,
+                    jnp.dot(attended[...], weight[k, :, cols], preferred_element_type=f32),
+                )
+
+        def store_own(cols, product):
+            own[c, :, cols] = product
+
+        def store_send(k, cols, product):
+            c_send[c, k, :, cols] = product.astype(bf16)
+
+        def store_joined(k, cols, product):
+            i = 2 - k
+            lower = slice(i * part_rows, (i + 1) * part_rows)
+            upper = slice((1 - i) * part_rows, (2 - i) * part_rows)
+            passed = c_recv[c, 3, lower, cols].astype(f32)
+            c_send[c, k, lower, cols] = (product[lower] + passed).astype(bf16)
+            c_send[c, k, upper, cols] = product[upper].astype(bf16)
+
+        if relay:
+            project(3, functools.partial(store_send, 3))
+            for i in range(2):
+                pass_c(c, i).start()
+            project(0, store_own)
+            for k in (1, 2):
+                pass_c(c, 2 - k).wait_recv()
+                project(k, functools.partial(store_joined, k))
+                send_c(c, k).start()
+        else:
+            @pl.loop(1, n)
+            def _(k):
+                project(k, functools.partial(store_send, k))
+                send_c(c, k).start()
+
+            project(0, store_own)
 
     for k in range(n):
         load_draft(k).wait()
@@ -312,19 +387,19 @@
 
     @pl.loop(0, chunks)
     def _(c):
-        for k in range(1, n):
+        for k in near:
             send_c(c, k).wait_recv()
         at = pl.ds(pl.multiple_of(c * span, span), span)
 
         def finish(j, squares):
             cols = pl.ds(pl.multiple_of(j * 128, 128), 128)
             total = own[c, :, cols]
-            for k in range(1, n):
+            for k in near:
                 total = total + c_recv[c, k, :, cols].astype(f32)
             feature = (residual_ref[at, cols].astype(f32) + total).astype(bf16)
             feature_ref[at, cols] = feature
             feature = feature.astype(f32)
-            scaled[:, cols] = (feature * gain_ref[:, cols].astype(f32)).astype(bf16)
+            scaled[:, cols] = (feature * gain[pl.ds(j, 1), :]).astype(bf16)
             return squares + feature * feature
 
         squares = lax.fori_loop(0, width // 128, finish, jnp.zeros((span, 128), f32))
@@ -372,8 +447,28 @@
     for k in range(1, n):
         send_t(k).wait_send()
         for c in range(chunks):
-            for send in (send_q, send_b, send_s, send_c, send_d, send_sq):
+            for send in (send_b, send_s, send_d, send_sq):
                 send(c, k).wait_send()
+    for c in range(chunks):
+        for k in near:
+            send_q(c, k).wait_send()
+            send_c(c, k).wait_send()
+        if relay:
+            for i in range(2):
+                forward_q(c, i).wait_send()
+                pass_c(c, i).wait_send()
+
+
+def hand_over(feature_ref, drafted_ref, feature_out, drafted_out, sems):
+    pairs = ((feature_ref, feature_out), (drafted_ref, drafted_out))
+    copies = [
+        pltpu.make_async_copy(source, target, sems.at[i])
+        for i, (source, target) in enumerate(pairs)
+    ]
+    for copy in copies:
+        copy.start()
+    for copy in copies:
+        copy.wait()
 
 
 def shards(
@@ -413,7 +508,7 @@
         pl.BlockSpec(memory_space=space) for space in (pltpu.VMEM, pltpu.SMEM, pl.ANY)
     )
     sems = dma((2, chunks, n))
-    return pl.pallas_call(
+    results = pl.pallas_call(
         functools.partial(kernel, n, chunks, groups),
         out_shape=(
             jax.ShapeDtypeStruct((rows, width), bf16),
@@ -444,6 +539,7 @@
             pltpu.VMEM((chunks, span, out_width), f32),
             pltpu.VMEM((chunks, 8, 128), f32),
             pltpu.VMEM((chunks, n, 8, 128), f32),
+            pltpu.VMEM((width // 128, 128), f32),
             dma,
             dma((n,)),
             dma((n,)),
@@ -468,11 +564,19 @@
         parents,
         tree_mask,
         residual,
-        norm_gain.reshape(1, -1),
+        norm_gain.reshape(-1, 128),
         cache_codes,
         output_weight,
         draft_weight,
     )
+    return pl.pallas_call(
+        hand_over,
+        out_shape=tuple(jax.ShapeDtypeStruct(one.shape, one.dtype) for one in results),
+        in_specs=[hbm, hbm],
+        out_specs=(hbm, hbm),
+        scratch_shapes=[dma((2,))],
+        compiler_params=pltpu.CompilerParams(vmem_limit_bytes=63 * 1024 * 1024),
+    )(*results)
 
 
 def solution(mesh):

time: 91.3 us -> 107 us (1.17)
  Pallas kernels: 85.7 us -> 106 us
  local copies, waits for them, and re-layouts: 4.74 us -> 0 us
    pallas_call x0 -> x1, Pallas kernels: none -> 21 us  [shards(): pl.pallas_call(hand_over, out_shape=tuple((jax.ShapeDtypeStruct(one.shape...]
    unnamed x2 -> x0, local copies, waits for them, and re-layouts: 3.45 us -> none
    reshape x1 -> x0, local copies, waits for them, and re-layouts: 1.29 us -> none  [shards(): norm_gain.reshape(1, -1)]
where the time goes in v2:
time: 107 us
  Pallas kernels  106 us (99%)
    pallas_call x1, Pallas kernels, shards(): pl.pallas_call(functools.partial(kernel, n, chunks, groups), out_shape=(j...  85.1 us
    pallas_call x1, Pallas kernels, shards(): pl.pallas_call(hand_over, out_shape=tuple((jax.ShapeDtypeStruct(one.shape...  21 us

profile of v2, /device:TPU:0, one launch (start us, length us, event | category | flops | bytes accessed | tf_op | source)
XLA Modules:
  0.0 106.8 jit_solution(18100526115974312379)
XLA Ops:
  0.6 85.1 %shard_map.140 = (bf16[128,2048]{1,0:T(8,128)(2,1)}, bf16[128,512]{1,0:T(8,128)(2,1)}) custom-call(bf16[128,2048]{1,0:T(8,128)(2,1)} %q_ref.1, bf16[32,2048]{1,0:T(8,128)(2,1)} %tree_ref.1, f32[20,8,2,128]{3,2,1,0:T(2,128)} %scales_ref.1, s32[8]{0:T(128)} %bits_ref.1, s32[4,20]{1,0:T(4,128)} %table_ref.1, s32[4]{0:T(128)} %lengths_ref.1, ...), custom_call_target="tpu_custom_call" | custom-call | tf_op jit(solution)/shard_map/pallas_call | solution.py:511
  85.8 21.0 %shard_map.141 = (bf16[128,2048]{1,0:T(8,128)(2,1)}, bf16[128,512]{1,0:T(8,128)(2,1)}) custom-call(bf16[128,2048]{1,0:T(8,128)(2,1)} %get-tuple-element.4.feature_ref, bf16[128,512]{1,0:T(8,128)(2,1)} %get-tuple-element.5.drafted_ref), custom_call_target="tpu_custom_call" | custom-call | tf_op jit(solution)/shard_map/pallas_call | solution.py:572

commit v3 on v2

--- a/solution.py
+++ b/solution.py
@@ -14,15 +14,22 @@
 
 
 def attend(stacked, keys, values, live, scale):
-    scores = lax.dot_general(
-        stacked, keys, (((1,), (1,)), ((), ())), preferred_element_type=jnp.float32
-    ) * scale
-    scores = jnp.where(live, scores, masked_score)
-    top = jnp.max(scores, axis=1, keepdims=True)
-    weights = jnp.where(live, jnp.exp(scores - top), 0.0)
-    total = jnp.sum(weights, axis=1, keepdims=True)
-    mixed = jnp.dot(weights.astype(jnp.bfloat16), values, preferred_element_type=jnp.float32)
-    return top, total, mixed / jnp.where(total > 0, total, 1.0)
+    floor = masked_score / scale
+    raw = lax.dot_general(
+        keys, stacked, (((1,), (1,)), ((), ())), preferred_element_type=jnp.float32
+    )
+    raw = jnp.where(live, raw, floor)
+    top = jnp.max(raw, axis=0, keepdims=True)
+    base = jnp.where(top == floor, 0.0, top)
+    weights = jnp.exp2((raw - base) * (scale * math.log2(math.e)))
+    total = jnp.sum(weights, axis=0, keepdims=True)
+    mixed = lax.dot_general(
+        values,
+        weights.astype(jnp.bfloat16),
+        (((0,), (0,)), ((), ())),
+        preferred_element_type=jnp.float32,
+    )
+    return top * scale, total, mixed * (1.0 / jnp.where(total > 0, total, 1.0))
 
 
 def kernel(
@@ -94,7 +101,7 @@
     tree_width = kv_dev * hd
     out_width = draft.shape[2]
     scale = 1.0 / math.sqrt(hd)
-    half = 128 // 2
+    lanes = gh * nodes
     f32, bf16 = jnp.float32, jnp.bfloat16
 
     relay = n == 4
@@ -212,21 +219,12 @@
                 codes = cache[slot, g, part].astype(f32)
                 cache[slot, g, part] = (ratio * (2.0 * codes - level + 1.0)).astype(bf16)
 
-    lane = lax.broadcasted_iota(jnp.int32, (nodes, 128), 1)
-    place = lax.broadcasted_iota(jnp.int32, (1, block), 1) + me * block
+    place = lax.broadcasted_iota(jnp.int32, (block, lanes), 0)
 
     def stack(c, k, r, j):
         at = slice(r * nodes, (r + 1) * nodes)
         cols = [slice((j * gh + h) * hd, (j * gh + h + 1) * hd) for h in range(gh)]
         return jnp.concatenate([q_all[c, k, at, col] for col in cols], axis=0)
-
-    def add_stats(stats, r, j, top, total):
-        for h in range(gh):
-            at = r * heads + j * gh + h
-            part = slice(h * nodes, (h + 1) * nodes)
-            stats = jnp.where(lane == at, top[part], stats)
-            stats = jnp.where(lane == half + at, total[part], stats)
-        return stats
 
     def receive_q(c):
         for k in (1, 2):
@@ -261,27 +259,20 @@
                     send_q(c, k).wait_recv()
 
             first = behind(k) * heads // groups
-            stats = jnp.zeros((nodes, 128), f32)
             for r in range(per):
                 request = c * per + r
                 ids = [table_ref[request, me * pages + p] for p in range(pages)]
-                live = place < lengths_ref[request]
+                live = place < lengths_ref[request] - me * block
                 for j in range(kv_dev):
+                    u = r * kv_dev + j
                     keys, values = (
                         jnp.concatenate([cache[i, first + j, part] for i in ids], axis=0)
                         for part in range(2)
                     )
                     top, total, mixed = attend(stack(c, k, r, j), keys, values, live, scale)
-                    stats = add_stats(stats, r, j, top, total)
-                    mixed = mixed.astype(bf16)
-                    for h in range(gh):
-                        b_send[
-                            c,
-                            k,
-                            r * nodes : (r + 1) * nodes,
-                            (j * gh + h) * hd : (j * gh + h + 1) * hd,
-                        ] = mixed[h * nodes : (h + 1) * nodes]
-            s_send[c, k] = stats
+                    s_send[c, k, 2 * u : 2 * u + 1, :] = top
+                    s_send[c, k, 2 * u + 1 : 2 * u + 2, :] = total
+                    b_send[c, k, u] = mixed.astype(bf16)
 
             @pl.when(k > 0)
             def _():
@@ -291,25 +282,29 @@
     for k in range(1, n):
         send_t(k).wait_recv()
 
+    turn_row = lax.broadcasted_iota(jnp.int32, (nodes, lanes), 0)
+    turn_lane = lax.broadcasted_iota(jnp.int32, (nodes, lanes), 1)
+    turn = (turn_row == lax.rem(turn_lane, nodes)).astype(f32).astype(bf16)
+
     @pl.loop(0, chunks)
     def _(c):
-        stats = jnp.zeros((nodes, 128), f32)
         for r in range(per):
             request = c * per + r
-            allowed = jnp.concatenate([mask_ref[request]] * gh, axis=0) > 0
+            turned = lax.dot_general(
+                mask_ref[request].astype(f32).astype(bf16),
+                turn,
+                (((0,), (0,)), ((), ())),
+                preferred_element_type=f32,
+            )
             at = pl.ds(pl.multiple_of(request * nodes, nodes), nodes)
             for j in range(kv_dev):
+                u = r * kv_dev + j
                 col = slice(j * hd, (j + 1) * hd)
                 keys, values = (t_all[part, at, col].astype(bf16) for part in range(2))
-                top, total, mixed = attend(stack(c, 0, r, j), keys, values, allowed, scale)
-                stats = add_stats(stats, r, j, top, total)
-                for h in range(gh):
-                    t_out[
-                        c,
-                        r * nodes : (r + 1) * nodes,
-                        (j * gh + h) * hd : (j * gh + h + 1) * hd,
-                    ] = mixed[h * nodes : (h + 1) * nodes]
-        t_stat[c] = stats
+                top, total, mixed = attend(stack(c, 0, r, j), keys, values, turned > 0.5, scale)
+                t_stat[c, 2 * u : 2 * u + 1, :] = top
+                t_stat[c, 2 * u + 1 : 2 * u + 2, :] = total
+                t_out[c, u] = mixed
 
     for k in range(n):
         load_weight(k).wait()
@@ -321,22 +316,26 @@
         for k in range(1, n):
             send_b(c, k).wait_recv()
             send_s(c, k).wait_recv()
-        stats = [t_stat[c], s_send[c, 0]] + [s_recv[c, k] for k in range(1, n)]
-        overall = functools.reduce(jnp.maximum, stats)
-        shares = [jnp.exp(one - overall) * pltpu.roll(one, half, 1) for one in stats]
-        inverse = 1.0 / functools.reduce(jnp.add, shares)
-        shares = [one * inverse for one in shares]
-        for r in range(per):
-            at = slice(r * nodes, (r + 1) * nodes)
-            for h in range(heads):
-                col = slice(h * hd, (h + 1) * hd)
-                i = r * heads + h
-                blocks = [t_out[c, at, col], b_send[c, 0, at, col].astype(f32)]
-                blocks += [b_recv[c, k, at, col].astype(f32) for k in range(1, n)]
-                mixed = functools.reduce(
-                    jnp.add, [one[:, i : i + 1] * b for one, b in zip(shares, blocks)]
-                )
-                attended[at, col] = mixed.astype(bf16)
+        for u in range(per * kv_dev):
+            tops, totals = (
+                [t_stat[c, row], s_send[c, 0, row]] + [s_recv[c, k, row] for k in range(1, n)]
+                for row in (slice(2 * u, 2 * u + 1), slice(2 * u + 1, 2 * u + 2))
+            )
+            overall = functools.reduce(jnp.maximum, tops)
+            shares = [jnp.exp(one - overall) * total for one, total in zip(tops, totals)]
+            inverse = 1.0 / functools.reduce(jnp.add, shares)
+            blocks = [t_out[c, u], b_send[c, 0, u].astype(f32)]
+            blocks += [b_recv[c, k, u].astype(f32) for k in range(1, n)]
+            mixed = functools.reduce(
+                jnp.add, [one * inverse * b for one, b in zip(shares, blocks)]
+            )
+            mixed = mixed.T.astype(bf16)
+            r, j = u // kv_dev, u % kv_dev
+            for h in range(gh):
+                attended[
+                    r * nodes : (r + 1) * nodes,
+                    (j * gh + h) * hd : (j * gh + h + 1) * hd,
+                ] = mixed[h * nodes : (h + 1) * nodes]
 
         def project(k, store):
             @pl.loop(0, width // tile)
@@ -459,16 +458,9 @@
                 pass_c(c, i).wait_send()
 
 
-def hand_over(feature_ref, drafted_ref, feature_out, drafted_out, sems):
-    pairs = ((feature_ref, feature_out), (drafted_ref, drafted_out))
-    copies = [
-        pltpu.make_async_copy(source, target, sems.at[i])
-        for i, (source, target) in enumerate(pairs)
-    ]
-    for copy in copies:
-        copy.start()
-    for copy in copies:
-        copy.wait()
+def hand_over(feature_ref, drafted_ref, feature_out, drafted_out):
+    feature_out[...] = feature_ref[...]
+    drafted_out[...] = drafted_ref[...]
 
 
 def shards(
@@ -495,10 +487,13 @@
     groups = query_heads // kv_heads
     heads = width // hd
     chunks = 2 if requests % 2 == 0 else 1
-    while requests // chunks * heads > 64 or requests // chunks * nodes > 128:
+    while requests // chunks * nodes > 128:
         chunks *= 2
     span = rows // chunks
     kv_dev = max(1, heads // groups)
+    units = requests // chunks * kv_dev
+    lanes = min(groups, heads) * nodes
+    stat_rows = -(-2 * units // 8) * 8
     tree_rows = tree_states.shape[0]
     wire = jnp.bfloat16 if tree_rows % 16 == 0 else jnp.float32
     out_width = draft_weight.shape[1] // n
@@ -523,12 +518,12 @@
             pltpu.VMEM((chunks, n, span, width), bf16),
             pltpu.VMEM((n, 2, tree_rows, kv_dev * hd), wire),
             pltpu.VMEM((2, rows, kv_dev * hd), wire),
-            pltpu.VMEM((chunks, n, span, width), bf16),
-            pltpu.VMEM((chunks, n, span, width), bf16),
-            pltpu.VMEM((chunks, n, nodes, 128), f32),
-            pltpu.VMEM((chunks, n, nodes, 128), f32),
-            pltpu.VMEM((chunks, span, width), f32),
-            pltpu.VMEM((chunks, nodes, 128), f32),
+            pltpu.VMEM((chunks, n, units, hd, lanes), bf16),
+            pltpu.VMEM((chunks, n, units, hd, lanes), bf16),
+            pltpu.VMEM((chunks, n, stat_rows, lanes), f32),
+            pltpu.VMEM((chunks, n, stat_rows, lanes), f32),
+            pltpu.VMEM((chunks, units, hd, lanes), f32),
+            pltpu.VMEM((chunks, stat_rows, lanes), f32),
             pltpu.VMEM((span, width), bf16),
             pltpu.VMEM((chunks, n, span, width), bf16),
             pltpu.VMEM((chunks, n, span, width), bf16),
@@ -572,9 +567,8 @@
     return pl.pallas_call(
         hand_over,
         out_shape=tuple(jax.ShapeDtypeStruct(one.shape, one.dtype) for one in results),
-        in_specs=[hbm, hbm],
-        out_specs=(hbm, hbm),
-        scratch_shapes=[dma((2,))],
+        in_specs=[vmem, vmem],
+        out_specs=(vmem, vmem),
         compiler_params=pltpu.CompilerParams(vmem_limit_bytes=63 * 1024 * 1024),
     )(*results)
 

time: 107 us -> 87.2 us (0.81)
  Pallas kernels: 106 us -> 86.4 us
    pallas_call x1, Pallas kernels: 21 us -> 1.93 us  [shards(): pl.pallas_call(hand_over, out_shape=tuple((jax.ShapeDtypeStruct(one.shape...]
where the time goes in v3:
time: 87.2 us; the launch traced here: 87 us
  Pallas kernels  86.4 us (99%)
    pallas_call x1, Pallas kernels, shards(): pl.pallas_call(functools.partial(kernel, n, chunks, groups), out_shape=(j...  84.5 us
    pallas_call x1, Pallas kernels, shards(): pl.pallas_call(hand_over, out_shape=tuple((jax.ShapeDtypeStruct(one.shape...  1.93 us

profile of v3, /device:TPU:0, one launch (start us, length us, event | category | flops | bytes accessed | tf_op | source)
XLA Modules:
  0.0 87.0 jit_solution(1237558732894356923)
XLA Ops:
  0.6 84.5 %shard_map.140 = (bf16[128,2048]{1,0:T(8,128)(2,1)}, bf16[128,512]{1,0:T(8,128)(2,1)}) custom-call(bf16[128,2048]{1,0:T(8,128)(2,1)} %q_ref.1, bf16[32,2048]{1,0:T(8,128)(2,1)} %tree_ref.1, f32[20,8,2,128]{3,2,1,0:T(2,128)} %scales_ref.1, s32[8]{0:T(128)} %bits_ref.1, s32[4,20]{1,0:T(4,128)} %table_ref.1, s32[4]{0:T(128)} %lengths_ref.1, ...), custom_call_target="tpu_custom_call" | custom-call | tf_op jit(solution)/shard_map/pallas_call | solution.py:506
  85.1 1.9 %shard_map.141 = (bf16[128,2048]{1,0:T(8,128)(2,1)}, bf16[128,512]{1,0:T(8,128)(2,1)}) custom-call(bf16[128,2048]{1,0:T(8,128)(2,1)} %get-tuple-element.4.feature_ref, bf16[128,512]{1,0:T(8,128)(2,1)} %get-tuple-element.5.drafted_ref), custom_call_target="tpu_custom_call" | custom-call | tf_op jit(solution)/shard_map/pallas_call | solution.py:567

commit v4 on v3

--- a/solution.py
+++ b/solution.py
@@ -106,6 +106,7 @@
 
     relay = n == 4
     part_rows = span // 2
+    part_units = b_send.shape[2] // 2
 
     def flipped(k):
         low = lax.rem(me + k, 2)
@@ -148,6 +149,15 @@
         return remote(
             c_send.at[c, 3, rows_at], c_recv.at[c, 3, rows_at], c_sems, (c, 3 - 3 * i), 1 + i
         )
+
+    def pass_b(c, i):
+        at = pl.ds(i * part_units, part_units)
+        return remote(
+            b_send.at[c, 3, at], b_recv.at[c, 3, at], b_sems, (c, 3 - 3 * i), 1 + i
+        )
+
+    def pass_s(c, i):
+        return remote(s_send.at[c, 3], s_recv.at[c, 3 - 3 * i], s_sems, (c, 3 - 3 * i), 1 + i)
 
     def send_t(k):
         at = pl.ds(pl.multiple_of(me * tree_rows, tree_rows), tree_rows)
@@ -211,13 +221,17 @@
 
     @pl.loop(0, slots)
     def _(slot):
-        for g in range(kv_heads):
-            level = jnp.full((1, hd), jnp.left_shift(jnp.int32(1), bits_ref[g]), jnp.int32)
-            level = level.astype(f32)
-            for part in range(2):
-                ratio = scales_ref[slot, g, part : part + 1, :] / level
-                codes = cache[slot, g, part].astype(f32)
-                cache[slot, g, part] = (ratio * (2.0 * codes - level + 1.0)).astype(bf16)
+        for g in range(0, kv_heads, 2):
+            codes, results = cache[slot, g : g + 2].astype(f32), []
+            for i in range(2):
+                level = jnp.full((1, hd), jnp.left_shift(jnp.int32(1), bits_ref[g + i]), jnp.int32)
+                level = level.astype(f32)
+                ratio = scales_ref[slot, g + i] / level
+                for part in range(2):
+                    centred = 2.0 * codes[i, part] - (level - 1.0)
+                    results.append((ratio[part : part + 1] * centred).astype(bf16))
+            for i, result in enumerate(results):
+                cache[slot, g + i // 2, i % 2] = result
 
     place = lax.broadcasted_iota(jnp.int32, (block, lanes), 0)
 
@@ -231,6 +245,27 @@
             send_q(c, k).wait_recv()
         for i in range(2):
             forward_q(c, i).start()
+
+    def merge(c):
+        for i in range(2):
+            pass_b(c, i).wait_recv()
+            pass_s(c, i).wait_recv()
+            k = 2 - i
+            for u in range(i * part_units, (i + 1) * part_units):
+                row, below = slice(2 * u, 2 * u + 1), slice(2 * u + 1, 2 * u + 2)
+                tops = s_send[c, k, row], s_recv[c, 3 - 3 * i, row]
+                overall = jnp.maximum(*tops)
+                first = jnp.exp(tops[0] - overall) * s_send[c, k, below]
+                other = jnp.exp(tops[1] - overall) * s_recv[c, 3 - 3 * i, below]
+                total = first + other
+                inverse = 1.0 / jnp.where(total > 0, total, 1.0)
+                mixed = (first * inverse) * b_send[c, k, u].astype(f32)
+                mixed = mixed + (other * inverse) * b_recv[c, 3, u].astype(f32)
+                b_send[c, k, u] = mixed.astype(bf16)
+                s_send[c, k, row] = overall
+                s_send[c, k, below] = total
+            send_b(c, k).start()
+            send_s(c, k).start()
 
     @pl.loop(0, chunks * n)
     def _(step):
@@ -250,6 +285,10 @@
                     @pl.when(c < chunks - 1)
                     def _():
                         receive_q(c + 1)
+
+                    @pl.when(c > 0)
+                    def _():
+                        merge(c - 1)
 
                     for i in range(2):
                         forward_q(c, i).wait_recv()
@@ -274,10 +313,17 @@
                     s_send[c, k, 2 * u + 1 : 2 * u + 2, :] = total
                     b_send[c, k, u] = mixed.astype(bf16)
 
-            @pl.when(k > 0)
-            def _():
-                send_b(c, back(k)).start()
-                send_s(c, back(k)).start()
+            if relay:
+                @pl.when(k == 3)
+                def _():
+                    for i in range(2):
+                        pass_b(c, i).start()
+                        pass_s(c, i).start()
+            else:
+                @pl.when(k > 0)
+                def _():
+                    send_b(c, back(k)).start()
+                    send_s(c, back(k)).start()
 
     for k in range(1, n):
         send_t(k).wait_recv()
@@ -306,6 +352,9 @@
                 t_stat[c, 2 * u + 1 : 2 * u + 2, :] = total
                 t_out[c, u] = mixed
 
+    if relay:
+        merge(chunks - 1)
+
     for k in range(n):
         load_weight(k).wait()
 
@@ -313,19 +362,19 @@
 
     @pl.loop(0, chunks)
     def _(c):
-        for k in range(1, n):
+        for k in near:
             send_b(c, k).wait_recv()
             send_s(c, k).wait_recv()
         for u in range(per * kv_dev):
             tops, totals = (
-                [t_stat[c, row], s_send[c, 0, row]] + [s_recv[c, k, row] for k in range(1, n)]
+                [t_stat[c, row], s_send[c, 0, row]] + [s_recv[c, k, row] for k in near]
                 for row in (slice(2 * u, 2 * u + 1), slice(2 * u + 1, 2 * u + 2))
             )
             overall = functools.reduce(jnp.maximum, tops)
             shares = [jnp.exp(one - overall) * total for one, total in zip(tops, totals)]
             inverse = 1.0 / functools.reduce(jnp.add, shares)
             blocks = [t_out[c, u], b_send[c, 0, u].astype(f32)]
-            blocks += [b_recv[c, k, u].astype(f32) for k in range(1, n)]
+            blocks += [b_recv[c, k, u].astype(f32) for k in near]
             mixed = functools.reduce(
                 jnp.add, [one * inverse * b for one, b in zip(shares, blocks)]
             )
@@ -446,15 +495,17 @@
     for k in range(1, n):
         send_t(k).wait_send()
         for c in range(chunks):
-            for send in (send_b, send_s, send_d, send_sq):
+            for send in (send_d, send_sq):
                 send(c, k).wait_send()
     for c in range(chunks):
         for k in near:
-            send_q(c, k).wait_send()
-            send_c(c, k).wait_send()
+            for send in (send_q, send_b, send_s, send_c):
+                send(c, k).wait_send()
         if relay:
             for i in range(2):
                 forward_q(c, i).wait_send()
+                pass_b(c, i).wait_send()
+                pass_s(c, i).wait_send()
                 pass_c(c, i).wait_send()
 
 

time: 87.2 us -> 80.3 us (0.921)
  Pallas kernels: 86.4 us -> 79.5 us
    pallas_call x1, Pallas kernels: 84.5 us -> 77.6 us  [shards(): pl.pallas_call(functools.partial(kernel, n, chunks, groups), out_shape=(j...]
where the time goes in v4:
time: 80.3 us; the launch traced here: 80.1 us
  Pallas kernels  79.5 us (99%)
    pallas_call x1, Pallas kernels, shards(): pl.pallas_call(functools.partial(kernel, n, chunks, groups), out_shape=(j...  77.6 us
    pallas_call x1, Pallas kernels, shards(): pl.pallas_call(hand_over, out_shape=tuple((jax.ShapeDtypeStruct(one.shape...  1.93 us

profile of v4, /device:TPU:0, one launch (start us, length us, event | category | flops | bytes accessed | tf_op | source)
XLA Modules:
  0.0 80.1 jit_solution(11835552310902508959)
XLA Ops:
  0.6 77.6 %shard_map.140 = (bf16[128,2048]{1,0:T(8,128)(2,1)}, bf16[128,512]{1,0:T(8,128)(2,1)}) custom-call(bf16[128,2048]{1,0:T(8,128)(2,1)} %q_ref.1, bf16[32,2048]{1,0:T(8,128)(2,1)} %tree_ref.1, f32[20,8,2,128]{3,2,1,0:T(2,128)} %scales_ref.1, s32[8]{0:T(128)} %bits_ref.1, s32[4,20]{1,0:T(4,128)} %table_ref.1, s32[4]{0:T(128)} %lengths_ref.1, ...), custom_call_target="tpu_custom_call" | custom-call | tf_op jit(solution)/shard_map/pallas_call | solution.py:557
  78.2 1.9 %shard_map.141 = (bf16[128,2048]{1,0:T(8,128)(2,1)}, bf16[128,512]{1,0:T(8,128)(2,1)}) custom-call(bf16[128,2048]{1,0:T(8,128)(2,1)} %get-tuple-element.4.feature_ref, bf16[128,512]{1,0:T(8,128)(2,1)} %get-tuple-element.5.drafted_ref), custom_call_target="tpu_custom_call" | custom-call | tf_op jit(solution)/shard_map/pallas_call | solution.py:618

commit v5 on v4

--- a/solution.py
+++ b/solution.py
@@ -207,11 +207,8 @@
     pl.semaphore_wait(barrier, n - 1)
 
     near = range(1, 3 if relay else n)
-    for c in range(chunks):
-        for k in near:
-            send_q(c, k).start()
-    for k in range(1, n):
-        send_t(k).start()
+    for k in near:
+        send_q(0, k).start()
     for k in range(n):
         load_weight(k).start()
     for k in range(n):
@@ -232,6 +229,12 @@
                     results.append((ratio[part : part + 1] * centred).astype(bf16))
             for i, result in enumerate(results):
                 cache[slot, g + i // 2, i % 2] = result
+
+    for c in range(1, chunks):
+        for k in near:
+            send_q(c, k).start()
+    for k in range(1, n):
+        send_t(k).start()
 
     place = lax.broadcasted_iota(jnp.int32, (block, lanes), 0)
 
@@ -276,16 +279,16 @@
 
         if n > 0:
             if relay:
-                @pl.when(step == chunks)
+                @pl.when(step == 1)
                 def _():
                     receive_q(0)
 
+                @pl.when((k == 2) & (c < chunks - 1))
+                def _():
+                    receive_q(c + 1)
+
                 @pl.when(k == 3)
                 def _():
-                    @pl.when(c < chunks - 1)
-                    def _():
-                        receive_q(c + 1)
-
                     @pl.when(c > 0)
                     def _():
                         merge(c - 1)

time: 80.3 us -> 80.3 us (level)
  no operation moved by 1% of the time
where the time goes in v5:
time: 80.3 us; the launch traced here: 80.1 us
  Pallas kernels  79.5 us (99%)
    pallas_call x1, Pallas kernels, shards(): pl.pallas_call(functools.partial(kernel, n, chunks, groups), out_shape=(j...  77.6 us
    pallas_call x1, Pallas kernels, shards(): pl.pallas_call(hand_over, out_shape=tuple((jax.ShapeDtypeStruct(one.shape...  1.93 us

profile of v5, /device:TPU:0, one launch (start us, length us, event | category | flops | bytes accessed | tf_op | source)
XLA Modules:
  0.0 80.1 jit_solution(2765443571290888850)
XLA Ops:
  0.6 77.6 %shard_map.140 = (bf16[128,2048]{1,0:T(8,128)(2,1)}, bf16[128,512]{1,0:T(8,128)(2,1)}) custom-call(bf16[128,2048]{1,0:T(8,128)(2,1)} %q_ref.1, bf16[32,2048]{1,0:T(8,128)(2,1)} %tree_ref.1, f32[20,8,2,128]{3,2,1,0:T(2,128)} %scales_ref.1, s32[8]{0:T(128)} %bits_ref.1, s32[4,20]{1,0:T(4,128)} %table_ref.1, s32[4]{0:T(128)} %lengths_ref.1, ...), custom_call_target="tpu_custom_call" | custom-call | tf_op jit(solution)/shard_map/pallas_call | solution.py:560
  78.2 1.9 %shard_map.141 = (bf16[128,2048]{1,0:T(8,128)(2,1)}, bf16[128,512]{1,0:T(8,128)(2,1)}) custom-call(bf16[128,2048]{1,0:T(8,128)(2,1)} %get-tuple-element.4.feature_ref, bf16[128,512]{1,0:T(8,128)(2,1)} %get-tuple-element.5.drafted_ref), custom_call_target="tpu_custom_call" | custom-call | tf_op jit(solution)/shard_map/pallas_call | solution.py:621

commit v6 on v5

--- a/solution.py
+++ b/solution.py
@@ -361,7 +361,7 @@
     for k in range(n):
         load_weight(k).wait()
 
-    tile = min(width, 512)
+    tile = min(width, 1024)
 
     @pl.loop(0, chunks)
     def _(c):

time: 80.3 us -> 79.5 us (0.990)
    pallas_call x1, Pallas kernels: 77.6 us -> 76.7 us  [shards(): pl.pallas_call(functools.partial(kernel, n, chunks, groups), out_shape=(j...]
where the time goes in v6:
time: 79.5 us; the launch traced here: 79.3 us
  Pallas kernels  78.7 us (99%)
    pallas_call x1, Pallas kernels, shards(): pl.pallas_call(functools.partial(kernel, n, chunks, groups), out_shape=(j...  76.7 us
    pallas_call x1, Pallas kernels, shards(): pl.pallas_call(hand_over, out_shape=tuple((jax.ShapeDtypeStruct(one.shape...  1.93 us

profile of v6, /device:TPU:0, one launch (start us, length us, event | category | flops | bytes accessed | tf_op | source)
XLA Modules:
  0.0 79.3 jit_solution(11082439504128966522)
XLA Ops:
  0.6 76.7 %shard_map.140 = (bf16[128,2048]{1,0:T(8,128)(2,1)}, bf16[128,512]{1,0:T(8,128)(2,1)}) custom-call(bf16[128,2048]{1,0:T(8,128)(2,1)} %q_ref.1, bf16[32,2048]{1,0:T(8,128)(2,1)} %tree_ref.1, f32[20,8,2,128]{3,2,1,0:T(2,128)} %scales_ref.1, s32[8]{0:T(128)} %bits_ref.1, s32[4,20]{1,0:T(4,128)} %table_ref.1, s32[4]{0:T(128)} %lengths_ref.1, ...), custom_call_target="tpu_custom_call" | custom-call | tf_op jit(solution)/shard_map/pallas_call | solution.py:560
  77.4 1.9 %shard_map.141 = (bf16[128,2048]{1,0:T(8,128)(2,1)}, bf16[128,512]{1,0:T(8,128)(2,1)}) custom-call(bf16[128,2048]{1,0:T(8,128)(2,1)} %get-tuple-element.4.feature_ref, bf16[128,512]{1,0:T(8,128)(2,1)} %get-tuple-element.5.drafted_ref), custom_call_target="tpu_custom_call" | custom-call | tf_op jit(solution)/shard_map/pallas_call | solution.py:621
